TPU v7x, 256 devices: a whole 4x4x8 slice. The times are simulated.
256 devices in a mesh: dp: 64 (over z, x, core), ctx: 4 (over y).
Axes of the slice: x: 4, y: 4, z: 8, core: 2. Of those that a mesh axis runs over, the one named last changes fastest.
Arguments:
- projected: bfloat16 [32768, 6144], P(('dp', 'ctx')), may hold values from -16 to 16
- out_grad: bfloat16 [32768, 2048], P(('dp', 'ctx')), may hold values from -6 to 6
- dest_row: int32 [32768], P(('dp', 'ctx')), may hold values from 0 to 32767, as said below
- lengths: int32 [64, 3], P('dp'), may hold values from 1 to 384, 512 in all within a row
Outputs:
- attended: bfloat16 [32768, 2048], P(('dp', 'ctx'))
- grad_projected: bfloat16 [32768, 6144], P(('dp', 'ctx'))
Inputs may be any that keep to these rules, and one draw needn't show every extreme that they name: Rollout rows move to dealt rows in aligned runs of 1; dest_row is a permutation of all rows; a row keeps its place along ctx: (dest_row[i] // 128) % 4 equals (i // 128) % 4; of the 128 rows of one device at most 3 go to one scorer group, and every device sends exactly 3 rows to some group.
All inputs are finite; a program needn't handle non-finite values.
Results may differ from a plain program's by a relative error of at most 0.007.
Values may be sent and summed in bfloat16 or wider, within the bound.
No kernel may reach another device: no remote copies, remote signals or barrier semaphores. Data moves between devices by JAX's collectives and lax.ppermute only.
A program may use at most 64 MiB of HBM per device.

v0:
```python
import math

import jax
import jax.numpy as jnp
from jax import lax
from jax.experimental import pallas as pl
from jax.experimental.pallas import tpu as pltpu
from jax.sharding import Mesh, PartitionSpec as P

DP = ("z", "x", "core")
HDIM = 128
SLOTS = 3
LOWEST = -1e30
MIB = 1024 * 1024


def swap_matrix(side):
    rows = lax.broadcasted_iota(jnp.int32, (side * side, side * side), 0)
    cols = lax.broadcasted_iota(jnp.int32, (side * side, side * side), 1)
    partner = (rows % side) * side + rows // side
    return (cols == partner).astype(jnp.bfloat16)


def iota(shape, axis):
    return lax.broadcasted_iota(jnp.int32, shape, axis)


def matmul(left, right):
    return jnp.dot(left, right, preferred_element_type=jnp.float32)


def matmul_nt(left, right):
    return lax.dot_general(
        left, right, (((1,), (1,)), ((), ())), preferred_element_type=jnp.float32
    )


def slot_of_rows(dest, groups, contexts, rows):
    target = dest // (rows * contexts)
    across = jnp.broadcast_to(target.astype(jnp.float32), (rows, rows))
    down = jnp.transpose(across)
    earlier = lax.broadcasted_iota(jnp.int32, (rows, rows), 0) < lax.broadcasted_iota(
        jnp.int32, (rows, rows), 1
    )
    same = jnp.where(jnp.logical_and(across == down, earlier), 1.0, 0.0)
    rank = jnp.sum(same, axis=0, keepdims=True).astype(jnp.int32)
    return rank * groups + target


def plan_kernel(groups, contexts, dest_ref, out_ref):
    rows = dest_ref.shape[1]
    planes = out_ref.shape[0]
    spots = groups // planes
    dest = dest_ref[...]
    slot = slot_of_rows(dest, groups, contexts, rows)
    group, rank = slot % groups, slot // groups
    local = (dest % rows + 1).astype(jnp.float32)
    held = jnp.where(iota((planes, rows), 0) == group // spots, local, 0.0)
    lanes = (iota((HDIM, rows), 0) == rank * spots + group % spots).astype(jnp.bfloat16)
    table = matmul_nt(held.astype(jnp.bfloat16), lanes).astype(jnp.int32)
    base = lax.axis_index("ctx") * rows
    out_ref[...] = jnp.where(table > 0, table + base, 0).reshape(out_ref.shape)


def pack_kernel(groups, contexts, proj_ref, cot_ref, dest_ref, out_ref, spread_ref, gone_ref, sem):
    rows = proj_ref.shape[0]
    width = cot_ref.shape[1]
    part = width // contexts
    pieces = 4 * part // HDIM
    slot = slot_of_rows(dest_ref[...], groups, contexts, rows)
    slots = SLOTS * groups
    pick = (iota((slots, rows), 0) == slot % groups * SLOTS + slot // groups).astype(jnp.bfloat16)
    departures = []
    for share in range(contexts):
        begin = share * part
        for t in range(4):
            source, at = (proj_ref, t * width + begin) if t < 3 else (cot_ref, begin)
            picked = matmul(pick, source[:, at : at + part])
            for k in range(part // HDIM):
                j = t * (part // HDIM) + k
                spread_ref[share % 2, pl.ds(j, slots, stride=pieces), :] = picked[
                    :, k * HDIM : (k + 1) * HDIM
                ]
        gone_ref[share] = (
            spread_ref[share % 2].astype(jnp.bfloat16).reshape(groups, SLOTS * pieces, HDIM)
        )
        departures.append(
            pltpu.make_async_copy(gone_ref.at[share], out_ref.at[:, share], sem.at[share])
        )
        departures[-1].start()
    for departure in departures:
        departure.wait()


def unpack_kernel(
    groups,
    contexts,
    in_ref,
    dest_ref,
    attended_ref,
    grad_ref,
    here_ref,
    gone_ref,
    in_sem,
    out_sem,
):
    rows, width = attended_ref.shape
    part = width // contexts
    pieces = 4 * part // HDIM
    arrivals = []
    for share in range(contexts):
        arrivals.append(
            pltpu.make_async_copy(in_ref.at[:, share], here_ref.at[share], in_sem.at[share])
        )
        arrivals[-1].start()
    slot = slot_of_rows(dest_ref[...], groups, contexts, rows)
    slots = SLOTS * groups
    slot_down = jnp.transpose(jnp.broadcast_to(slot.astype(jnp.float32), (rows, rows)))[:, :1]
    pick = (iota((rows, slots), 1) == slot_down.astype(jnp.int32)).astype(jnp.bfloat16)
    swap = swap_matrix(pieces)
    departures = []
    for share in range(contexts):
        arrivals[share].wait()
        stacked = []
        for rank in range(SLOTS):
            chunks = jnp.concatenate(
                [
                    here_ref[
                        share, first : first + pieces, rank * pieces : (rank + 1) * pieces, :
                    ].reshape(pieces * pieces, HDIM)
                    for first in range(0, groups, pieces)
                ],
                axis=1,
            )
            swapped = matmul(swap, chunks).astype(jnp.bfloat16)
            for at in range(groups // pieces):
                stacked.append(
                    jnp.concatenate(
                        [
                            swapped[j * pieces : (j + 1) * pieces, at * HDIM : (at + 1) * HDIM]
                            for j in range(pieces)
                        ],
                        axis=1,
                    )
                )
        result = matmul(pick, jnp.concatenate(stacked, axis=0)).astype(jnp.bfloat16)
        begin = share * part
        for t in range(4):
            gone_ref[share, t] = result[:, t * part : (t + 1) * part]
            target, at = (grad_ref, (t - 1) * width + begin) if t else (attended_ref, begin)
            target = target.at[:, pl.ds(at, part)]
            departures.append(
                pltpu.make_async_copy(gone_ref.at[share, t], target, out_sem.at[share, t])
            )
            departures[-1].start()
    for departure in departures:
        departure.wait()


def attend_kernel(
    in_ref,
    place_ref,
    lengths_ref,
    out_ref,
    here_ref,
    slot_ref,
    row_ref,
    back_ref,
    gone_ref,
    in_sem,
    out_sem,
):
    groups, contexts, lines, _ = in_ref.shape
    pieces = lines // SLOTS
    heads = pieces // 4
    rows = row_ref.shape[0] // contexts
    spots = lax.axis_size("x") * lax.axis_size("core")
    arrivals = []
    for context in range(contexts):
        arrivals.append(
            pltpu.make_async_copy(
                in_ref.at[:, context], here_ref.at[context], in_sem.at[context]
            )
        )
        arrivals[-1].start()
    swap = swap_matrix(pieces)

    scatters, gathers = [], []
    for context in range(contexts):
        downs, acrosses = [], []
        for rank in range(SLOTS):
            lane = rank * spots + lax.axis_index("x") * lax.axis_size("core")
            lane = lane + lax.axis_index("core")
            place = place_ref[context].astype(jnp.float32)
            place = jnp.where(iota((groups, HDIM), 1) == lane, place, 0.0)
            down = jnp.sum(place, axis=1, keepdims=True) - (context * rows + 1.0)
            downs.append(down.astype(jnp.int32))
            spread = jnp.broadcast_to(down, (groups, HDIM))
            acrosses.append(jnp.transpose(spread)[:1, :])
        place_down = jnp.concatenate(downs, axis=0)
        place_across = jnp.concatenate(acrosses, axis=1).astype(jnp.int32)
        slots = SLOTS * groups
        gathers.append((iota((rows, slots), 0) == place_across).astype(jnp.bfloat16))
        scatters.append((iota((slots, rows), 1) == place_down).astype(jnp.bfloat16))

    end0 = lengths_ref[0, 0]
    end1 = end0 + lengths_ref[0, 1]
    end2 = end1 + lengths_ref[0, 2]

    def segment(axis):
        position = iota((contexts * rows, contexts * rows), axis)
        return (
            (position >= end0).astype(jnp.int32)
            + (position >= end1).astype(jnp.int32)
            + (position >= end2).astype(jnp.int32)
        )

    bias = jnp.where(segment(0) == segment(1), 0.0, LOWEST)

    for context in range(contexts):
        arrivals[context].wait()
        for rank in range(SLOTS):
            chunks = jnp.concatenate(
                [
                    here_ref[
                        context, first : first + pieces, rank * pieces : (rank + 1) * pieces, :
                    ].reshape(pieces * pieces, HDIM)
                    for first in range(0, groups, pieces)
                ],
                axis=1,
            )
            swapped = matmul(swap, chunks).astype(jnp.bfloat16)
            for at in range(groups // pieces):
                begin = rank * groups + at * pieces
                for j in range(pieces):
                    slot_ref[context, begin : begin + pieces, j * HDIM : (j + 1) * HDIM] = swapped[
                        j * pieces : (j + 1) * pieces, at * HDIM : (at + 1) * HDIM
                    ]
        row_ref[context * rows : (context + 1) * rows, :] = matmul(
            gathers[context], slot_ref[context]
        ).astype(jnp.bfloat16)

    scale = 1.0 / math.sqrt(HDIM)
    for head in range(heads):
        query, key, value, cotangent = [
            row_ref[:, (t * heads + head) * HDIM : (t * heads + head + 1) * HDIM]
            for t in range(4)
        ]
        scores = matmul_nt(key, query) * (scale * math.log2(math.e)) + bias
        top = jnp.max(scores, axis=0, keepdims=True)
        powers = jnp.exp2(scores - top)
        total = jnp.sum(powers, axis=0, keepdims=True)
        exact = powers * (1.0 / total)
        weights = exact.astype(jnp.bfloat16)
        mixed = matmul(jnp.transpose(value), weights)
        drift = jnp.sum(
            jnp.transpose(cotangent).astype(jnp.float32) * mixed, axis=0, keepdims=True
        )
        pulls = matmul_nt(value, cotangent)
        slopes = (exact * ((pulls - drift) * scale)).astype(jnp.bfloat16)
        query_grad = matmul(jnp.transpose(key), slopes)
        key_grad = matmul(slopes, query)
        value_grad = matmul(weights, cotangent)
        by_query = jnp.concatenate([mixed, query_grad], axis=0).astype(jnp.bfloat16)
        by_key = jnp.concatenate([key_grad, value_grad], axis=1).astype(jnp.bfloat16)
        for context in range(contexts):
            span = slice(context * rows, (context + 1) * rows)
            results = (
                matmul_nt(scatters[context], by_query[:, span]),
                matmul(scatters[context], by_key[span, :]),
            )
            for t in range(4):
                j = t * heads + head
                back_ref[context, :, j * HDIM : (j + 1) * HDIM] = results[t // 2][
                    :, t % 2 * HDIM : (t % 2 + 1) * HDIM
                ].astype(jnp.bfloat16)

    departures = []
    for context in range(contexts):
        for rank in range(SLOTS):
            chunks = []
            for first in range(rank * groups, (rank + 1) * groups, pieces):
                chunks.append(
                    jnp.concatenate(
                        [
                            back_ref[context, first : first + pieces, j * HDIM : (j + 1) * HDIM]
                            for j in range(pieces)
                        ],
                        axis=0,
                    )
                )
            swapped = matmul(swap, jnp.concatenate(chunks, axis=1)).astype(jnp.bfloat16)
            for at in range(groups // pieces):
                gone_ref[
                    context, at * pieces : (at + 1) * pieces, rank * pieces : (rank + 1) * pieces, :
                ] = swapped[:, at * HDIM : (at + 1) * HDIM].reshape(pieces, pieces, HDIM)
        departures.append(
            pltpu.make_async_copy(
                gone_ref.at[context], out_ref.at[:, context], out_sem.at[context]
            )
        )
        departures[-1].start()
    for departure in departures:
        departure.wait()


def call_pack(groups, contexts, projected, out_grad, dest):
    lanes = 4 * out_grad.shape[1] // contexts
    pieces = lanes // HDIM
    whole = pl.BlockSpec(memory_space=pltpu.VMEM)
    return pl.pallas_call(
        lambda *refs: pack_kernel(groups, contexts, *refs),
        out_shape=jax.ShapeDtypeStruct((groups, contexts, SLOTS * pieces, HDIM), jnp.bfloat16),
        in_specs=[whole] * 3,
        out_specs=pl.BlockSpec(memory_space=pl.ANY),
        scratch_shapes=[
            pltpu.VMEM((2, SLOTS * groups * pieces, HDIM), jnp.float32),
            pltpu.VMEM((contexts, groups, SLOTS * pieces, HDIM), jnp.bfloat16),
            pltpu.SemaphoreType.DMA((contexts,)),
        ],
        compiler_params=pltpu.CompilerParams(vmem_limit_bytes=56 * MIB),
        name="pack",
    )(projected, out_grad, dest)


def call_plan(groups, contexts, planes, dest):
    whole = pl.BlockSpec(memory_space=pltpu.VMEM)
    return pl.pallas_call(
        lambda *refs: plan_kernel(groups, contexts, *refs),
        out_shape=jax.ShapeDtypeStruct((planes, 1, HDIM), jnp.int32),
        in_specs=[whole],
        out_specs=whole,
        compiler_params=pltpu.CompilerParams(vmem_limit_bytes=8 * MIB),
        name="plan",
    )(dest)


def call_attend(contexts, rows, arrived, places, lengths):
    devices, lines, _ = arrived.shape
    groups = devices // contexts
    lanes = lines // SLOTS * HDIM
    whole = pl.BlockSpec(memory_space=pltpu.VMEM)
    far = pl.BlockSpec(memory_space=pl.ANY)
    blocks = pltpu.VMEM((contexts, groups, lines, HDIM), jnp.bfloat16)
    slots = pltpu.VMEM((contexts, SLOTS * groups, lanes), jnp.bfloat16)
    return pl.pallas_call(
        attend_kernel,
        out_shape=jax.ShapeDtypeStruct((groups, contexts, lines, HDIM), jnp.bfloat16),
        in_specs=[far, whole, pl.BlockSpec(memory_space=pltpu.SMEM)],
        out_specs=far,
        scratch_shapes=[
            blocks,
            slots,
            pltpu.VMEM((contexts * rows, lanes), jnp.bfloat16),
            slots,
            blocks,
            pltpu.SemaphoreType.DMA((contexts,)),
            pltpu.SemaphoreType.DMA((contexts,)),
        ],
        compiler_params=pltpu.CompilerParams(vmem_limit_bytes=36 * MIB),
        name="attend",
    )(arrived.reshape(groups, contexts, lines, HDIM), places, lengths)


def call_unpack(groups, contexts, returned, dest):
    rows = dest.shape[1]
    lines = returned.shape[2]
    part = lines // (SLOTS * 4) * HDIM
    width = contexts * part
    whole = pl.BlockSpec(memory_space=pltpu.VMEM)
    far = pl.BlockSpec(memory_space=pl.ANY)
    return pl.pallas_call(
        lambda *refs: unpack_kernel(groups, contexts, *refs),
        out_shape=(
            jax.ShapeDtypeStruct((rows, width), jnp.bfloat16),
            jax.ShapeDtypeStruct((rows, 3 * width), jnp.bfloat16),
        ),
        in_specs=[far, whole],
        out_specs=(far, far),
        scratch_shapes=[
            pltpu.VMEM((contexts, groups, lines, HDIM), jnp.bfloat16),
            pltpu.VMEM((contexts, 4, rows, part), jnp.bfloat16),
            pltpu.SemaphoreType.DMA((contexts,)),
            pltpu.SemaphoreType.DMA((contexts, 4)),
        ],
        compiler_params=pltpu.CompilerParams(vmem_limit_bytes=20 * MIB),
        name="unpack",
    )(returned, dest)


def on_device(projected, out_grad, dest_row, lengths):
    rows = out_grad.shape[0]
    planes, contexts = lax.axis_size("z"), lax.axis_size("ctx")
    groups = lax.axis_size(DP)
    everyone = DP + ("ctx",)
    dest = dest_row.reshape(1, rows)

    plan = call_plan(groups, contexts, planes, dest)
    plan = lax.all_to_all(plan, "z", 0, 0, tiled=True).reshape(planes, HDIM)
    sent = call_pack(groups, contexts, projected, out_grad, dest)
    lines = sent.shape[2]
    arrived = lax.all_to_all(sent.reshape(-1, lines, HDIM), everyone, 0, 0, tiled=True)
    places = plan
    for axis in ("ctx", "core", "x"):
        places = lax.all_gather(places, axis, axis=0)
    places = jnp.transpose(places, (2, 3, 0, 1, 4)).reshape(contexts, groups, HDIM)
    answers = call_attend(contexts, rows, arrived, places, lengths)
    returned = lax.all_to_all(
        answers.reshape(-1, lines, HDIM), everyone, 0, 0, tiled=True
    )
    return call_unpack(
        groups, contexts, returned.reshape(groups, contexts, lines, HDIM), dest
    )


def solution(mesh):
    parts = Mesh(mesh.devices.reshape(8, 4, 2, -1), DP + ("ctx",))
    everyone = DP + ("ctx",)
    return jax.shard_map(
        on_device,
        mesh=parts,
        in_specs=(P(everyone, None), P(everyone, None), P(everyone), P(DP, None)),
        out_specs=(P(everyone, None), P(everyone, None)),
        check_vma=False,
    )
```

profile of v0, /device:TPU:1, one launch (start us, length us, event | category | flops | bytes accessed | tf_op | source)
XLA Modules:
  0.0 204.3 jit_solution(990034560984944821)
XLA Ops:
  0.6 0.0 copy-start
  0.6 0.6 copy-done
  1.3 0.9 plan.1
  2.2 9.0 %all-to-all-start.1 = ((s32[8,1,128]{2,1,0:T(1,128)}), s32[8,1,128]{2,1,0:T(1,128)S(1)}, u32[]{:S(2)}, u32[]{:S(2)}) async-start(s32[8,1,128]{2,1,0:T(1,128)} %plan.1), calls=%async_computation.1 | async-start | bytes 8192 | tf_op jit(solution)/shard_map/all_to_all | solution.py:399
  11.2 5.2 %pack.1 = bf16[64,4,48,128]{3,2,1,0:T(8,128)(2,1)} custom-call(bf16[128,6144]{1,0:T(8,128)(2,1)} %refs_0_.1, bf16[128,2048]{1,0:T(8,128)(2,1)} %refs_1_.1, s32[1,128]{1,0:T(1,128)} %bitcast.15), custom_call_target="tpu_custom_call" | custom-call | tf_op jit(solution)/shard_map/pack/pallas_call | solution.py:311
  16.4 1.3 all-to-all-done.1
  17.6 0.0 copy-start.2
  17.6 12.6 %all-to-all-start = ((bf16[256,48,128]{2,1,0:T(8,128)(2,1)}), bf16[256,48,128]{2,1,0:T(8,128)(2,1)S(1)}, u32[]{:S(2)}, u32[]{:S(2)}) async-start(bf16[256,48,128]{2,1,0:T(8,128)(2,1)} %bitcast.18), calls=%async_computation | async-start | bytes 6291456 | tf_op jit(solution)/shard_map/all_to_all | solution.py:402
  30.3 10.7 %all-gather = s32[32,1,128]{2,1,0:T(1,128)S(1)} all-gather(s32[8,1,128]{2,1,0:T(1,128)S(1)} %all-to-all-done.1), channel_id=2, replica_groups=mesh['z'=8,'x'=4,'core'=2,'ctx'=4] {'ctx'}, dimensions={0}, use_global_device_ids=true | all-gather | bytes 20480 | tf_op jit(solution)/shard_map/all_gather | solution.py:405
  40.9 7.4 %all-gather.1 = s32[8,8,128]{2,1,0:T(8,128)S(1)} all-gather(s32[4,8,128]{2,1,0:T(8,128)S(1)} %bitcast.21), channel_id=3, replica_groups=mesh['z'=8,'x'=4,'core'=2,'ctx'=4] {'core'}, dimensions={0}, use_global_device_ids=true | all-gather | bytes 49152 | tf_op jit(solution)/shard_map/all_gather | solution.py:405
  48.4 10.6 %all-gather.2 = s32[8,4,8,128]{3,2,1,0:T(8,128)S(1)} all-gather(s32[2,4,8,128]{3,2,1,0:T(8,128)S(1)} %bitcast.20), channel_id=4, replica_groups=mesh['z'=8,'x'=4,'core'=2,'ctx'=4] {'x'}, dimensions={0}, use_global_device_ids=true | all-gather | bytes 163840 | tf_op jit(solution)/shard_map/all_gather | solution.py:405
  59.0 0.1 copy.7
  59.1 47.2 %all-to-all-done = bf16[256,48,128]{2,1,0:T(8,128)(2,1)S(1)} async-done(((bf16[256,48,128]{2,1,0:T(8,128)(2,1)}), bf16[256,48,128]{2,1,0:T(8,128)(2,1)S(1)}, u32[]{:S(2)}, u32[]{:S(2)}) %all-to-all-start) | async-done | bytes 3145760 | tf_op jit(solution)/shard_map/all_to_all | solution.py:402
  106.2 0.0 copy-done.2
  106.2 11.7 %attend.1 = bf16[64,4,48,128]{3,2,1,0:T(8,128)(2,1)S(1)} custom-call(bf16[64,4,48,128]{3,2,1,0:T(8,128)(2,1)S(1)} %bitcast.11, s32[4,64,128]{2,1,0:T(8,128)S(1)} %bitcast.14, s32[1,3]{1,0:T(1,128)S(1)} %copy-done.2), custom_call_target="tpu_custom_call" | custom-call | tf_op jit(solution)/shard_map/attend/pallas_call | solution.py:346
  117.9 0.0 copy-start.1
  117.9 82.2 %all_to_all.15 = bf16[256,48,128]{2,1,0:T(8,128)(2,1)S(1)} all-to-all(bf16[256,48,128]{2,1,0:T(8,128)(2,1)S(1)} %bitcast.13), channel_id=1, replica_groups=mesh['z'=8,'x'=4,'core'=2,'ctx'=4] {'z','x','core','ctx'}, dimensions={0} | all-to-all | bytes 6291456 | tf_op jit(solution)/shard_map/all_to_all | solution.py:408
  200.2 0.0 copy-done.1
  200.2 4.0 %unpack.1 = (bf16[128,2048]{1,0:T(8,128)(2,1)}, bf16[128,6144]{1,0:T(8,128)(2,1)}) custom-call(bf16[64,4,48,128]{3,2,1,0:T(8,128)(2,1)S(1)} %bitcast.12, s32[1,128]{1,0:T(1,128)S(1)} %bitcast.17), custom_call_target="tpu_custom_call" | custom-call | tf_op jit(solution)/shard_map/unpack/pallas_call | solution.py:372
Async XLA Ops:
  0.6 0.7 copy-start
  2.2 15.5 %all-to-all-start.1 = ((s32[8,1,128]{2,1,0:T(1,128)}), s32[8,1,128]{2,1,0:T(1,128)S(1)}, u32[]{:S(2)}, u32[]{:S(2)}) async-start(s32[8,1,128]{2,1,0:T(1,128)} %plan.1), calls=%async_computation.1 | async-start | bytes 8192 | tf_op jit(solution)/shard_map/all_to_all | solution.py:399
  17.6 88.6 %copy-start.2 = (s32[1,3]{1,0:T(1,128)S(1)}, s32[1,3]{1,0:T(1,128)}, u32[]{:S(2)}) copy-start(s32[1,3]{1,0:T(1,128)} %lengths_ref.1) | copy-start | bytes 40
  17.6 88.6 %all-to-all-start = ((bf16[256,48,128]{2,1,0:T(8,128)(2,1)}), bf16[256,48,128]{2,1,0:T(8,128)(2,1)S(1)}, u32[]{:S(2)}, u32[]{:S(2)}) async-start(bf16[256,48,128]{2,1,0:T(8,128)(2,1)} %bitcast.18), calls=%async_computation | async-start | bytes 6291456 | tf_op jit(solution)/shard_map/all_to_all | solution.py:402
  117.9 82.2 %copy-start.1 = (s32[128]{0:T(128)S(1)}, s32[128]{0:T(128)}, u32[]{:S(2)}) copy-start(s32[128]{0:T(128)} %param.6) | copy-start | bytes 1540
where the time goes:
time: 205 us; the launch traced here: 204 us
  blocking collectives  111 us (54%)
  waiting for transfers between devices  48.4 us (24%)
  Pallas kernels  21.8 us (11%)
  starting transfers between devices  21.6 us (11%)
    all_to_all x1, blocking collectives, on_device(): lax.all_to_all(answers.reshape(-1, lines, HDIM), everyone, 0, 0, tiled=True)  82.2 us
    all_to_all x1, waiting for transfers between devices, on_device(): lax.all_to_all(sent.reshape(-1, lines, HDIM), everyone, 0, 0, tiled=True)  47.2 us
    all_gather x3, blocking collectives, on_device(): places = lax.all_gather(places, axis, axis=0)  28.7 us
    all_to_all x1, starting transfers between devices, on_device(): lax.all_to_all(sent.reshape(-1, lines, HDIM), everyone, 0, 0, tiled=True)  12.6 us
    pallas_call x1, Pallas kernels, call_attend(): pl.pallas_call(attend_kernel, out_shape=jax.ShapeDtypeStruct((groups, con...  11.7 us
    all_to_all x1, starting transfers between devices, on_device(): plan = lax.all_to_all(plan, 'z', 0, 0, tiled=True).reshape(planes, HDIM)  9.01 us
    pallas_call x1, Pallas kernels, call_pack(): pl.pallas_call(lambda *refs: pack_kernel(groups, contexts, *refs), out_sh...  5.19 us
  transfers between devices with their start and end apart: 2, of which 2 were waited for; matrix products, arithmetic and copies ran while one was open for 0% of the time, Pallas kernels for 3%

commit v1 on v0

--- a/solution.py
+++ b/solution.py
@@ -99,20 +99,12 @@
     dest_ref,
     attended_ref,
     grad_ref,
-    here_ref,
     gone_ref,
-    in_sem,
     out_sem,
 ):
     rows, width = attended_ref.shape
     part = width // contexts
     pieces = 4 * part // HDIM
-    arrivals = []
-    for share in range(contexts):
-        arrivals.append(
-            pltpu.make_async_copy(in_ref.at[:, share], here_ref.at[share], in_sem.at[share])
-        )
-        arrivals[-1].start()
     slot = slot_of_rows(dest_ref[...], groups, contexts, rows)
     slots = SLOTS * groups
     slot_down = jnp.transpose(jnp.broadcast_to(slot.astype(jnp.float32), (rows, rows)))[:, :1]
@@ -120,13 +112,12 @@
     swap = swap_matrix(pieces)
     departures = []
     for share in range(contexts):
-        arrivals[share].wait()
         stacked = []
         for rank in range(SLOTS):
             chunks = jnp.concatenate(
                 [
-                    here_ref[
-                        share, first : first + pieces, rank * pieces : (rank + 1) * pieces, :
+                    in_ref[
+                        first : first + pieces, share, rank * pieces : (rank + 1) * pieces, :
                     ].reshape(pieces * pieces, HDIM)
                     for first in range(0, groups, pieces)
                 ],
@@ -162,12 +153,10 @@
     place_ref,
     lengths_ref,
     out_ref,
-    here_ref,
     slot_ref,
     row_ref,
     back_ref,
     gone_ref,
-    in_sem,
     out_sem,
 ):
     groups, contexts, lines, _ = in_ref.shape
@@ -175,14 +164,6 @@
     heads = pieces // 4
     rows = row_ref.shape[0] // contexts
     spots = lax.axis_size("x") * lax.axis_size("core")
-    arrivals = []
-    for context in range(contexts):
-        arrivals.append(
-            pltpu.make_async_copy(
-                in_ref.at[:, context], here_ref.at[context], in_sem.at[context]
-            )
-        )
-        arrivals[-1].start()
     swap = swap_matrix(pieces)
 
     scatters, gathers = [], []
@@ -218,12 +199,11 @@
     bias = jnp.where(segment(0) == segment(1), 0.0, LOWEST)
 
     for context in range(contexts):
-        arrivals[context].wait()
         for rank in range(SLOTS):
             chunks = jnp.concatenate(
                 [
-                    here_ref[
-                        context, first : first + pieces, rank * pieces : (rank + 1) * pieces, :
+                    in_ref[
+                        first : first + pieces, context, rank * pieces : (rank + 1) * pieces, :
                     ].reshape(pieces * pieces, HDIM)
                     for first in range(0, groups, pieces)
                 ],
@@ -346,15 +326,13 @@
     return pl.pallas_call(
         attend_kernel,
         out_shape=jax.ShapeDtypeStruct((groups, contexts, lines, HDIM), jnp.bfloat16),
-        in_specs=[far, whole, pl.BlockSpec(memory_space=pltpu.SMEM)],
+        in_specs=[whole, whole, pl.BlockSpec(memory_space=pltpu.SMEM)],
         out_specs=far,
         scratch_shapes=[
-            blocks,
             slots,
             pltpu.VMEM((contexts * rows, lanes), jnp.bfloat16),
             slots,
             blocks,
-            pltpu.SemaphoreType.DMA((contexts,)),
             pltpu.SemaphoreType.DMA((contexts,)),
         ],
         compiler_params=pltpu.CompilerParams(vmem_limit_bytes=36 * MIB),
@@ -375,12 +353,10 @@
             jax.ShapeDtypeStruct((rows, width), jnp.bfloat16),
             jax.ShapeDtypeStruct((rows, 3 * width), jnp.bfloat16),
         ),
-        in_specs=[far, whole],
+        in_specs=[whole, whole],
         out_specs=(far, far),
         scratch_shapes=[
-            pltpu.VMEM((contexts, groups, lines, HDIM), jnp.bfloat16),
             pltpu.VMEM((contexts, 4, rows, part), jnp.bfloat16),
-            pltpu.SemaphoreType.DMA((contexts,)),
             pltpu.SemaphoreType.DMA((contexts, 4)),
         ],
         compiler_params=pltpu.CompilerParams(vmem_limit_bytes=20 * MIB),

time: 205 us -> 202 us (0.985)
  Pallas kernels: 21.8 us -> 18.7 us
where the time goes in v1:
time: 202 us; the launch traced here: 201 us
  blocking collectives  111 us (55%)
  waiting for transfers between devices  48.4 us (24%)
  starting transfers between devices  21.6 us (11%)
  Pallas kernels  18.7 us (9%)
    all_to_all x1, blocking collectives, on_device(): lax.all_to_all(answers.reshape(-1, lines, HDIM), everyone, 0, 0, tiled=True)  82.2 us
    all_to_all x1, waiting for transfers between devices, on_device(): lax.all_to_all(sent.reshape(-1, lines, HDIM), everyone, 0, 0, tiled=True)  47.2 us
    all_gather x3, blocking collectives, on_device(): places = lax.all_gather(places, axis, axis=0)  28.7 us
    all_to_all x1, starting transfers between devices, on_device(): lax.all_to_all(sent.reshape(-1, lines, HDIM), everyone, 0, 0, tiled=True)  12.6 us
    pallas_call x1, Pallas kernels, call_attend(): pl.pallas_call(attend_kernel, out_shape=jax.ShapeDtypeStruct((groups, con...  9.82 us
    all_to_all x1, starting transfers between devices, on_device(): plan = lax.all_to_all(plan, 'z', 0, 0, tiled=True).reshape(planes, HDIM)  9.01 us
    pallas_call x1, Pallas kernels, call_pack(): pl.pallas_call(lambda *refs: pack_kernel(groups, contexts, *refs), out_sh...  5.19 us
  transfers between devices with their start and end apart: 2, of which 2 were waited for; matrix products, arithmetic and copies ran while one was open for 0% of the time, Pallas kernels for 3%

profile of v1, /device:TPU:1, one launch (start us, length us, event | category | flops | bytes accessed | tf_op | source)
XLA Modules:
  0.0 201.2 jit_solution(12044978111130857567)
XLA Ops:
  0.6 0.0 copy-start
  0.6 0.6 copy-done
  1.3 0.9 plan.1
  2.2 9.0 %all-to-all-start.1 = ((s32[8,1,128]{2,1,0:T(1,128)}), s32[8,1,128]{2,1,0:T(1,128)S(1)}, u32[]{:S(2)}, u32[]{:S(2)}) async-start(s32[8,1,128]{2,1,0:T(1,128)} %plan.1), calls=%async_computation.1 | async-start | bytes 8192 | tf_op jit(solution)/shard_map/all_to_all | solution.py:375
  11.2 5.2 %pack.1 = bf16[64,4,48,128]{3,2,1,0:T(8,128)(2,1)} custom-call(bf16[128,6144]{1,0:T(8,128)(2,1)} %refs_0_.1, bf16[128,2048]{1,0:T(8,128)(2,1)} %refs_1_.1, s32[1,128]{1,0:T(1,128)} %bitcast.15), custom_call_target="tpu_custom_call" | custom-call | tf_op jit(solution)/shard_map/pack/pallas_call | solution.py:291
  16.4 1.3 all-to-all-done.1
  17.6 0.0 copy-start.2
  17.6 12.6 %all-to-all-start = ((bf16[256,48,128]{2,1,0:T(8,128)(2,1)}), bf16[256,48,128]{2,1,0:T(8,128)(2,1)S(1)}, u32[]{:S(2)}, u32[]{:S(2)}) async-start(bf16[256,48,128]{2,1,0:T(8,128)(2,1)} %bitcast.18), calls=%async_computation | async-start | bytes 6291456 | tf_op jit(solution)/shard_map/all_to_all | solution.py:378
  30.3 10.7 %all-gather = s32[32,1,128]{2,1,0:T(1,128)S(1)} all-gather(s32[8,1,128]{2,1,0:T(1,128)S(1)} %all-to-all-done.1), channel_id=2, replica_groups=mesh['z'=8,'x'=4,'core'=2,'ctx'=4] {'ctx'}, dimensions={0}, use_global_device_ids=true | all-gather | bytes 20480 | tf_op jit(solution)/shard_map/all_gather | solution.py:381
  40.9 7.4 %all-gather.1 = s32[8,8,128]{2,1,0:T(8,128)S(1)} all-gather(s32[4,8,128]{2,1,0:T(8,128)S(1)} %bitcast.21), channel_id=3, replica_groups=mesh['z'=8,'x'=4,'core'=2,'ctx'=4] {'core'}, dimensions={0}, use_global_device_ids=true | all-gather | bytes 49152 | tf_op jit(solution)/shard_map/all_gather | solution.py:381
  48.4 10.6 %all-gather.2 = s32[8,4,8,128]{3,2,1,0:T(8,128)S(1)} all-gather(s32[2,4,8,128]{3,2,1,0:T(8,128)S(1)} %bitcast.20), channel_id=4, replica_groups=mesh['z'=8,'x'=4,'core'=2,'ctx'=4] {'x'}, dimensions={0}, use_global_device_ids=true | all-gather | bytes 163840 | tf_op jit(solution)/shard_map/all_gather | solution.py:381
  59.0 0.1 copy.7
  59.1 47.2 %all-to-all-done = bf16[256,48,128]{2,1,0:T(8,128)(2,1)S(1)} async-done(((bf16[256,48,128]{2,1,0:T(8,128)(2,1)}), bf16[256,48,128]{2,1,0:T(8,128)(2,1)S(1)}, u32[]{:S(2)}, u32[]{:S(2)}) %all-to-all-start) | async-done | bytes 3145760 | tf_op jit(solution)/shard_map/all_to_all | solution.py:378
  106.2 0.0 copy-done.2
  106.2 9.8 %attend.1 = bf16[64,4,48,128]{3,2,1,0:T(8,128)(2,1)S(1)} custom-call(bf16[64,4,48,128]{3,2,1,0:T(8,128)(2,1)S(1)} %bitcast.11, s32[4,64,128]{2,1,0:T(8,128)S(1)} %bitcast.14, s32[1,3]{1,0:T(1,128)S(1)} %copy-done.2), custom_call_target="tpu_custom_call" | custom-call | tf_op jit(solution)/shard_map/attend/pallas_call | solution.py:326
  116.1 0.0 copy-start.1
  116.1 82.2 %all_to_all.15 = bf16[256,48,128]{2,1,0:T(8,128)(2,1)S(1)} all-to-all(bf16[256,48,128]{2,1,0:T(8,128)(2,1)S(1)} %bitcast.13), channel_id=1, replica_groups=mesh['z'=8,'x'=4,'core'=2,'ctx'=4] {'z','x','core','ctx'}, dimensions={0} | all-to-all | bytes 6291456 | tf_op jit(solution)/shard_map/all_to_all | solution.py:384
  198.3 0.0 copy-done.1
  198.3 2.8 %unpack.1 = (bf16[128,2048]{1,0:T(8,128)(2,1)}, bf16[128,6144]{1,0:T(8,128)(2,1)}) custom-call(bf16[64,4,48,128]{3,2,1,0:T(8,128)(2,1)S(1)} %bitcast.12, s32[1,128]{1,0:T(1,128)S(1)} %bitcast.17), custom_call_target="tpu_custom_call" | custom-call | tf_op jit(solution)/shard_map/unpack/pallas_call | solution.py:350
Async XLA Ops:
  0.6 0.7 copy-start
  2.2 15.5 %all-to-all-start.1 = ((s32[8,1,128]{2,1,0:T(1,128)}), s32[8,1,128]{2,1,0:T(1,128)S(1)}, u32[]{:S(2)}, u32[]{:S(2)}) async-start(s32[8,1,128]{2,1,0:T(1,128)} %plan.1), calls=%async_computation.1 | async-start | bytes 8192 | tf_op jit(solution)/shard_map/all_to_all | solution.py:375
  17.6 88.6 %copy-start.2 = (s32[1,3]{1,0:T(1,128)S(1)}, s32[1,3]{1,0:T(1,128)}, u32[]{:S(2)}) copy-start(s32[1,3]{1,0:T(1,128)} %lengths_ref.1) | copy-start | bytes 40
  17.6 88.6 %all-to-all-start = ((bf16[256,48,128]{2,1,0:T(8,128)(2,1)}), bf16[256,48,128]{2,1,0:T(8,128)(2,1)S(1)}, u32[]{:S(2)}, u32[]{:S(2)}) async-start(bf16[256,48,128]{2,1,0:T(8,128)(2,1)} %bitcast.18), calls=%async_computation | async-start | bytes 6291456 | tf_op jit(solution)/shard_map/all_to_all | solution.py:378
  116.1 82.2 %copy-start.1 = (s32[128]{0:T(128)S(1)}, s32[128]{0:T(128)}, u32[]{:S(2)}) copy-start(s32[128]{0:T(128)} %param.6) | copy-start | bytes 1540

commit v2 on v1

--- a/solution.py
+++ b/solution.py
@@ -62,28 +62,40 @@
     out_ref[...] = jnp.where(table > 0, table + base, 0).reshape(out_ref.shape)
 
 
-def pack_kernel(groups, contexts, proj_ref, cot_ref, dest_ref, out_ref, spread_ref, gone_ref, sem):
+def pack_kernel(groups, contexts, proj_ref, cot_ref, dest_ref, out_ref, gone_ref, sem):
     rows = proj_ref.shape[0]
     width = cot_ref.shape[1]
     part = width // contexts
     pieces = 4 * part // HDIM
     slot = slot_of_rows(dest_ref[...], groups, contexts, rows)
     slots = SLOTS * groups
-    pick = (iota((slots, rows), 0) == slot % groups * SLOTS + slot // groups).astype(jnp.bfloat16)
+    pick = (iota((slots, rows), 0) == slot).astype(jnp.bfloat16)
+    swap = swap_matrix(pieces)
     departures = []
     for share in range(contexts):
         begin = share * part
+        picked = []
         for t in range(4):
             source, at = (proj_ref, t * width + begin) if t < 3 else (cot_ref, begin)
-            picked = matmul(pick, source[:, at : at + part])
-            for k in range(part // HDIM):
-                j = t * (part // HDIM) + k
-                spread_ref[share % 2, pl.ds(j, slots, stride=pieces), :] = picked[
-                    :, k * HDIM : (k + 1) * HDIM
-                ]
-        gone_ref[share] = (
-            spread_ref[share % 2].astype(jnp.bfloat16).reshape(groups, SLOTS * pieces, HDIM)
-        )
+            picked.append(matmul(pick, source[:, at : at + part]).astype(jnp.bfloat16))
+        picked = jnp.concatenate(picked, axis=1)
+        for rank in range(SLOTS):
+            chunks = []
+            for first in range(rank * groups, (rank + 1) * groups, pieces):
+                chunks.append(
+                    jnp.concatenate(
+                        [
+                            picked[first : first + pieces, j * HDIM : (j + 1) * HDIM]
+                            for j in range(pieces)
+                        ],
+                        axis=0,
+                    )
+                )
+            swapped = matmul(swap, jnp.concatenate(chunks, axis=1)).astype(jnp.bfloat16)
+            for at in range(groups // pieces):
+                gone_ref[
+                    share, at * pieces : (at + 1) * pieces, rank * pieces : (rank + 1) * pieces, :
+                ] = swapped[:, at * HDIM : (at + 1) * HDIM].reshape(pieces, pieces, HDIM)
         departures.append(
             pltpu.make_async_copy(gone_ref.at[share], out_ref.at[:, share], sem.at[share])
         )
@@ -294,7 +306,6 @@
         in_specs=[whole] * 3,
         out_specs=pl.BlockSpec(memory_space=pl.ANY),
         scratch_shapes=[
-            pltpu.VMEM((2, SLOTS * groups * pieces, HDIM), jnp.float32),
             pltpu.VMEM((contexts, groups, SLOTS * pieces, HDIM), jnp.bfloat16),
             pltpu.SemaphoreType.DMA((contexts,)),
         ],

time: 202 us -> 201 us (level)
  transfers between devices with their start and end apart: 2 -> 2, of which waited for: 2 -> 2; matrix products, arithmetic and copies ran while one was open for 0% -> 0% of each run, Pallas kernels for 3% -> 2%
where the time goes in v2:
time: 201 us
  blocking collectives  111 us (55%)
  waiting for transfers between devices  48.7 us (24%)
  starting transfers between devices  21.3 us (11%)
  Pallas kernels  18.3 us (9%)
    all_to_all x1, blocking collectives, on_device(): lax.all_to_all(answers.reshape(-1, lines, HDIM), everyone, 0, 0, tiled=True)  82.2 us
    all_to_all x1, waiting for transfers between devices, on_device(): lax.all_to_all(sent.reshape(-1, lines, HDIM), everyone, 0, 0, tiled=True)  47.2 us
    all_gather x3, blocking collectives, on_device(): places = lax.all_gather(places, axis, axis=0)  28.7 us
    all_to_all x1, starting transfers between devices, on_device(): lax.all_to_all(sent.reshape(-1, lines, HDIM), everyone, 0, 0, tiled=True)  12.3 us
    pallas_call x1, Pallas kernels, call_attend(): pl.pallas_call(attend_kernel, out_shape=jax.ShapeDtypeStruct((groups, con...  9.81 us
    all_to_all x1, starting transfers between devices, on_device(): plan = lax.all_to_all(plan, 'z', 0, 0, tiled=True).reshape(planes, HDIM)  9.01 us
    pallas_call x1, Pallas kernels, call_pack(): pl.pallas_call(lambda *refs: pack_kernel(groups, contexts, *refs), out_sh...  4.88 us
  transfers between devices with their start and end apart: 2, of which 2 were waited for; matrix products, arithmetic and copies ran while one was open for 0% of the time, Pallas kernels for 2%

profile of v2, /device:TPU:1, one launch (start us, length us, event | category | flops | bytes accessed | tf_op | source)
XLA Modules:
  0.0 200.9 jit_solution(813466407428910624)
XLA Ops:
  0.6 0.0 copy-start
  0.6 0.6 copy-done
  1.3 0.9 plan.1
  2.2 9.0 %all-to-all-start.1 = ((s32[8,1,128]{2,1,0:T(1,128)}), s32[8,1,128]{2,1,0:T(1,128)S(1)}, u32[]{:S(2)}, u32[]{:S(2)}) async-start(s32[8,1,128]{2,1,0:T(1,128)} %plan.1), calls=%async_computation.1 | async-start | bytes 8192 | tf_op jit(solution)/shard_map/all_to_all | solution.py:386
  11.2 4.9 %pack.1 = bf16[64,4,48,128]{3,2,1,0:T(8,128)(2,1)} custom-call(bf16[128,6144]{1,0:T(8,128)(2,1)} %refs_0_.1, bf16[128,2048]{1,0:T(8,128)(2,1)} %refs_1_.1, s32[1,128]{1,0:T(1,128)} %bitcast.15), custom_call_target="tpu_custom_call" | custom-call | tf_op jit(solution)/shard_map/pack/pallas_call | solution.py:303
  16.1 1.6 all-to-all-done.1
  17.6 0.0 copy-start.2
  17.6 12.3 %all-to-all-start = ((bf16[256,48,128]{2,1,0:T(8,128)(2,1)}), bf16[256,48,128]{2,1,0:T(8,128)(2,1)S(1)}, u32[]{:S(2)}, u32[]{:S(2)}) async-start(bf16[256,48,128]{2,1,0:T(8,128)(2,1)} %bitcast.18), calls=%async_computation | async-start | bytes 6291456 | tf_op jit(solution)/shard_map/all_to_all | solution.py:389
  30.0 10.7 %all-gather = s32[32,1,128]{2,1,0:T(1,128)S(1)} all-gather(s32[8,1,128]{2,1,0:T(1,128)S(1)} %all-to-all-done.1), channel_id=2, replica_groups=mesh['z'=8,'x'=4,'core'=2,'ctx'=4] {'ctx'}, dimensions={0}, use_global_device_ids=true | all-gather | bytes 20480 | tf_op jit(solution)/shard_map/all_gather | solution.py:392
  40.6 7.4 %all-gather.1 = s32[8,8,128]{2,1,0:T(8,128)S(1)} all-gather(s32[4,8,128]{2,1,0:T(8,128)S(1)} %bitcast.21), channel_id=3, replica_groups=mesh['z'=8,'x'=4,'core'=2,'ctx'=4] {'core'}, dimensions={0}, use_global_device_ids=true | all-gather | bytes 49152 | tf_op jit(solution)/shard_map/all_gather | solution.py:392
  48.1 10.6 %all-gather.2 = s32[8,4,8,128]{3,2,1,0:T(8,128)S(1)} all-gather(s32[2,4,8,128]{3,2,1,0:T(8,128)S(1)} %bitcast.20), channel_id=4, replica_groups=mesh['z'=8,'x'=4,'core'=2,'ctx'=4] {'x'}, dimensions={0}, use_global_device_ids=true | all-gather | bytes 163840 | tf_op jit(solution)/shard_map/all_gather | solution.py:392
  58.7 0.1 copy.7
  58.8 47.2 %all-to-all-done = bf16[256,48,128]{2,1,0:T(8,128)(2,1)S(1)} async-done(((bf16[256,48,128]{2,1,0:T(8,128)(2,1)}), bf16[256,48,128]{2,1,0:T(8,128)(2,1)S(1)}, u32[]{:S(2)}, u32[]{:S(2)}) %all-to-all-start) | async-done | bytes 3145760 | tf_op jit(solution)/shard_map/all_to_all | solution.py:389
  105.9 0.0 copy-done.2
  105.9 9.8 %attend.1 = bf16[64,4,48,128]{3,2,1,0:T(8,128)(2,1)S(1)} custom-call(bf16[64,4,48,128]{3,2,1,0:T(8,128)(2,1)S(1)} %bitcast.11, s32[4,64,128]{2,1,0:T(8,128)S(1)} %bitcast.14, s32[1,3]{1,0:T(1,128)S(1)} %copy-done.2), custom_call_target="tpu_custom_call" | custom-call | tf_op jit(solution)/shard_map/attend/pallas_call | solution.py:337
  115.8 0.0 copy-start.1
  115.8 82.2 %all_to_all.15 = bf16[256,48,128]{2,1,0:T(8,128)(2,1)S(1)} all-to-all(bf16[256,48,128]{2,1,0:T(8,128)(2,1)S(1)} %bitcast.13), channel_id=1, replica_groups=mesh['z'=8,'x'=4,'core'=2,'ctx'=4] {'z','x','core','ctx'}, dimensions={0} | all-to-all | bytes 6291456 | tf_op jit(solution)/shard_map/all_to_all | solution.py:395
  198.0 0.0 copy-done.1
  198.0 2.8 %unpack.1 = (bf16[128,2048]{1,0:T(8,128)(2,1)}, bf16[128,6144]{1,0:T(8,128)(2,1)}) custom-call(bf16[64,4,48,128]{3,2,1,0:T(8,128)(2,1)S(1)} %bitcast.12, s32[1,128]{1,0:T(1,128)S(1)} %bitcast.17), custom_call_target="tpu_custom_call" | custom-call | tf_op jit(solution)/shard_map/unpack/pallas_call | solution.py:361
Async XLA Ops:
  0.6 0.7 copy-start
  2.2 15.5 %all-to-all-start.1 = ((s32[8,1,128]{2,1,0:T(1,128)}), s32[8,1,128]{2,1,0:T(1,128)S(1)}, u32[]{:S(2)}, u32[]{:S(2)}) async-start(s32[8,1,128]{2,1,0:T(1,128)} %plan.1), calls=%async_computation.1 | async-start | bytes 8192 | tf_op jit(solution)/shard_map/all_to_all | solution.py:386
  17.6 88.3 %copy-start.2 = (s32[1,3]{1,0:T(1,128)S(1)}, s32[1,3]{1,0:T(1,128)}, u32[]{:S(2)}) copy-start(s32[1,3]{1,0:T(1,128)} %lengths_ref.1) | copy-start | bytes 40
  17.6 88.3 %all-to-all-start = ((bf16[256,48,128]{2,1,0:T(8,128)(2,1)}), bf16[256,48,128]{2,1,0:T(8,128)(2,1)S(1)}, u32[]{:S(2)}, u32[]{:S(2)}) async-start(bf16[256,48,128]{2,1,0:T(8,128)(2,1)} %bitcast.18), calls=%async_computation | async-start | bytes 6291456 | tf_op jit(solution)/shard_map/all_to_all | solution.py:389
  115.8 82.2 %copy-start.1 = (s32[128]{0:T(128)S(1)}, s32[128]{0:T(128)}, u32[]{:S(2)}) copy-start(s32[128]{0:T(128)} %param.6) | copy-start | bytes 1540
